TPU v7x, 256 devices: a whole 4x4x8 slice. The times are simulated.
256 devices in a mesh: rep: 64 (over y, z, x_lo), fsdp: 4 (over x_hi, core).
Axes of the slice: x: 4 (x_hi: 2, x_lo: 2; x = x_hi * 2 + x_lo), y: 4, z: 8, core: 2. Of those that a mesh axis runs over, the one named last changes fastest.
Arguments:
- hidden_in: bfloat16 [64, 1024, 4096], P('rep', 'fsdp'), may hold values from -36 to 36
- norm_gain: float32 [4096], replicated, may hold values from 0.1 to 1.9
- replica_weight: bfloat16 [64, 4096, 512], P('rep', 'fsdp'), may hold values from -8.8 to 8.8
- cotangent: bfloat16 [64, 1024, 512], P('rep', 'fsdp'), may hold values from -12 to 12
- adam_first: float32 [64, 4096, 512], P('rep', 'fsdp'), may hold values from -3 to 3
- adam_second: float32 [64, 4096, 512], P('rep', 'fsdp'), may hold values from 0.1 to 4
- anchor: float32 [4096, 512], P(('fsdp', 'rep')), may hold values from -4 to 4
- outer_momentum: float32 [4096, 512], P(('fsdp', 'rep')), may hold values from -1.8 to 1.8
Outputs:
- projected: bfloat16 [64, 1024, 512], P('rep', 'fsdp')
- first_moment: float32 [64, 4096, 512], P('rep', 'fsdp')
- second_moment: float32 [64, 4096, 512], P('rep', 'fsdp')
- new_anchor: float32 [4096, 512], P(('fsdp', 'rep'))
- new_momentum: float32 [4096, 512], P(('fsdp', 'rep'))
All inputs are finite; a program needn't handle non-finite values.
Results may differ from a plain program's by a relative error of at most 0.0049.
Values may be sent and summed in bfloat16 or wider, within the bound.
A program may use at most 64 MiB of HBM per device.

v0:
```python
import jax
import jax.numpy as jnp
from jax import lax
from jax.sharding import PartitionSpec as P

beta_one = 0.9
beta_two = 0.95
adam_eps = 1e-08
inner_rate = 0.02
decay_rate = 0.1
nesterov_mu = 0.9
outer_rate = 0.7


def per_device(
    hidden_in, norm_gain, replica_weight, cotangent, adam_first, adam_second, anchor, outer_momentum
):
    tokens = hidden_in[0]
    weights = replica_weight[0]
    grad_out = cotangent[0]
    inv_root = tokens.shape[1] ** (-0.5)
    weights32 = weights.astype(jnp.float32)
    wide = tokens.astype(jnp.float32)
    square = jnp.mean(wide * wide, axis=-1, keepdims=True)
    normed = (wide * lax.rsqrt(square + 1e-05) * norm_gain).astype(jnp.bfloat16)
    columns = normed
    accumulated = jnp.dot(
        columns,
        lax.all_gather(weights, "fsdp", axis=0, tiled=True),
        preferred_element_type=jnp.float32,
    )
    projected = (accumulated * inv_root).astype(jnp.bfloat16)
    columns = normed
    gradient = lax.psum_scatter(
        (
            jnp.einsum("td,tk->dk", columns, grad_out, preferred_element_type=jnp.float32)
            * inv_root
        ).astype(jnp.bfloat16),
        "fsdp",
        scatter_dimension=0,
        tiled=True,
    ).astype(jnp.float32)
    moment_one = beta_one * adam_first[0] + (1.0 - beta_one) * gradient
    moment_two = beta_two * adam_second[0] + (1.0 - beta_two) * gradient * gradient
    adam_step = moment_one / (jnp.sqrt(moment_two) + adam_eps) + decay_rate * weights32
    updated = weights32 - inner_rate * adam_step
    replicas = lax.axis_size("rep")
    share_rows = anchor.shape[0]
    full_anchor = lax.all_gather(anchor, "rep", axis=0, tiled=True)
    summed = lax.psum(full_anchor - updated, "rep")
    rep_index = lax.axis_index("rep")
    mean_delta = lax.dynamic_slice_in_dim(summed, rep_index * share_rows, share_rows, 0) / replicas
    new_momentum = nesterov_mu * outer_momentum + mean_delta
    new_anchor = anchor - outer_rate * (nesterov_mu * new_momentum + mean_delta)
    return (projected[None], moment_one[None], moment_two[None], new_anchor, new_momentum)


def solution(mesh):
    placed = (
        P("rep", "fsdp", None),
        P(),
        P("rep", "fsdp", None),
        P("rep", "fsdp", None),
        P("rep", "fsdp", None),
        P("rep", "fsdp", None),
        P(("fsdp", "rep"), None),
        P(("fsdp", "rep"), None),
    )
    return jax.shard_map(
        per_device,
        mesh=mesh,
        in_specs=placed,
        out_specs=(
            P("rep", "fsdp", None),
            P("rep", "fsdp", None),
            P("rep", "fsdp", None),
            P(("fsdp", "rep"), None),
            P(("fsdp", "rep"), None),
        ),
        check_vma=False,
    )
```

profile of v0, /device:TPU:2, one launch (start us, length us, event | category | flops | bytes accessed | tf_op | source)
XLA Modules:
  0.0 989.9 jit_solution(10068022324874972719)
XLA Ops:
  8.0 0.0 copy-start
  8.0 0.0 copy-start.3
  8.0 0.0 copy-start.7
  8.0 0.0 all-gather.4.cloned.1.call-start
  8.1 0.7 all-gather.4.cloned.1.call-update
  8.8 0.0 reduce-scatter.2.cloned.1.call-start
  8.8 2.1 fusion.2
  10.9 0.0 copy-done
  10.9 0.0 copy-done.3
  10.9 0.0 copy-done.7
  10.9 3.5 multiply_convert_fusion
  14.5 0.0 copy-start.1
  14.5 0.0 copy-start.2
  14.5 0.0 reduce-scatter.2.cloned.1.call-update
  14.5 0.0 all-gather.6.cloned.1.call-start
  14.5 0.7 all-gather.6.cloned.1.call-update
  15.2 0.0 all-reduce.2.cloned.1.call-start
  15.3 315.2 %all-gather.4.cloned.1.call-done = f32[1024,512]{1,0:T(8,128)} async-done(((f32[16,512]{1,0:T(8,128)}), f32[1024,512]{1,0:T(8,128)}) %all-gather.4.cloned.1.call-update) | async-done | bytes 2097168 | tf_op jit(solution)/shard_map/all_gather | solution.py:49
  330.4 0.0 reduce-scatter.2.cloned.1.call-done
  330.4 0.0 copy-done.1
  330.4 0.0 copy-done.2
  330.4 6.4 fusion.12
  336.9 0.0 copy-start.4
  336.9 0.0 all-reduce.2.cloned.1.call-update
  336.9 0.0 copy-start.5
  336.9 0.0 copy-start.6
  336.9 33.2 %all-gather.6.cloned.1.call-done = bf16[1,4096,512]{2,1,0:T(8,128)(2,1)} async-done(((bf16[1,1024,512]{2,1,0:T(8,128)(2,1)}), bf16[1,4096,512]{2,1,0:T(8,128)(2,1)}) %all-gather.6.cloned.1.call-update) | async-done | bytes 4194320 | tf_op jit(solution)/shard_map/all_gather | solution.py:29
  370.1 0.0 copy-done.4
  370.1 4.2 fusion.32
  374.3 607.1 %all-reduce.2.cloned.1.call-done = f32[1024,512]{1,0:T(8,128)} async-done(((f32[1024,512]{1,0:T(8,128)}), f32[1024,512]{1,0:T(8,128)}) %all-reduce.2.cloned.1.call-update) | async-done | bytes 2097168 | tf_op jit(solution)/shard_map/psum | solution.py:50
  981.4 0.0 copy-done.5
  981.4 0.0 copy-done.6
  981.4 1.4 multiply_subtract_fusion
  (1 shorter events, 0.0 us)
Async XLA Ops:
  8.0 2.9 copy-start
  8.0 2.9 copy-start.3
  8.0 2.9 copy-start.7
  8.0 322.4 %all-gather.4.cloned.1.call-start = ((), (), s32[]{:S(2)}) async-start(), calls=%async_computation.2 | async-start | bytes 2129920 | tf_op jit(solution)/shard_map/all_gather | solution.py:49
  8.8 321.7 %reduce-scatter.2.cloned.1.call-start = ((), (), s32[]{:S(2)}) async-start(), calls=%async_computation.1 | async-start | bytes 5242880 | tf_op jit(solution)/shard_map/reduce_scatter | solution.py:34
  14.5 316.0 %copy-start.1 = (bf16[1,1024,512]{2,1,0:T(8,128)(2,1)S(1)}, bf16[1,1024,512]{2,1,0:T(8,128)(2,1)}, u32[]{:S(2)}) copy-start(bf16[1,1024,512]{2,1,0:T(8,128)(2,1)} %param.10) | copy-start | bytes 3145732
  14.5 316.0 %copy-start.2 = (f32[1,1024,512]{2,1,0:T(8,128)S(1)}, f32[1,1024,512]{2,1,0:T(8,128)}, u32[]{:S(2)}) copy-start(f32[1,1024,512]{2,1,0:T(8,128)} %param.12) | copy-start | bytes 6291460
  14.5 355.6 %all-gather.6.cloned.1.call-start = ((), (), s32[]{:S(2)}) async-start(), calls=%async_computation.4 | async-start | bytes 5242880 | tf_op jit(solution)/shard_map/all_gather | solution.py:29
  15.2 966.1 %all-reduce.2.cloned.1.call-start = ((), (), s32[]{:S(2)}) async-start(), calls=%async_computation.3 | async-start | bytes 4194304 | tf_op jit(solution)/shard_map/psum | solution.py:50
  336.9 33.2 %copy-start.4 = (bf16[1,256,4096]{2,1,0:T(8,128)(2,1)S(1)}, bf16[1,256,4096]{2,1,0:T(8,128)(2,1)}, u32[]{:S(2)}) copy-start(bf16[1,256,4096]{2,1,0:T(8,128)(2,1)} %param.8) | copy-start | bytes 6291460
  336.9 644.5 %copy-start.5 = (f32[16,512]{1,0:T(8,128)S(1)}, f32[16,512]{1,0:T(8,128)}, u32[]{:S(2)}) copy-start(f32[16,512]{1,0:T(8,128)} %param.14) | copy-start | bytes 98308
  336.9 644.5 %copy-start.6 = (f32[16,512]{1,0:T(8,128)S(1)}, f32[16,512]{1,0:T(8,128)}, u32[]{:S(2)}) copy-start(f32[16,512]{1,0:T(8,128)} %param.15) | copy-start | bytes 98308
Sparse Core Ops, SparseCore 0:
  10.7 319.7 all-gather.3
  332.3 37.7 all-gather.5
  372.9 608.4 all-reduce.1
Sparse Core Ops, SparseCore 1:
  14.6 59.3 reduce-scatter.1
where the time goes:
time: 991 us; the launch traced here: 990 us
  waiting for transfers between devices  957 us (97%)
  between operations  15.3 us (2%)
    psum x1, waiting for transfers between devices, per_device(): summed = lax.psum(full_anchor - updated, 'rep')  607 us
    all_gather x1, waiting for transfers between devices, per_device(): full_anchor = lax.all_gather(anchor, 'rep', axis=0, tiled=True)  315 us
    all_gather x1, waiting for transfers between devices, per_device(): lax.all_gather(weights, 'fsdp', axis=0, tiled=True)  33.2 us
  transfers between devices with their start and end apart: 4, of which 3 were waited for; matrix products, arithmetic and copies ran while one was open for 2% of the time, Pallas kernels for 0%

commit v1 on v0

v1 whole, which is shorter than its diff:
```python
import jax
import jax.numpy as jnp
from jax import lax
from jax.experimental import pallas as pl
from jax.experimental.pallas import tpu as pltpu
from jax.sharding import PartitionSpec as P

MESH = pl.DeviceIdType.MESH
BF, F32 = jnp.bfloat16, jnp.float32

beta_one = 0.9
beta_two = 0.95
adam_eps = 1e-08
inner_rate = 0.02
decay_rate = 0.1
nesterov_mu = 0.9
outer_rate = 0.7

NY, NZ, REPLICAS = 4, 8, 64
DIST = (4, 3, 5, 2, 6, 1, 7, 0)
AHEAD = 3
LAG = 2
KV = 512


def contract_first(a, b):
    return lax.dot_general(a, b, (((0,), (0,)), ((), ())), preferred_element_type=F32)


def kernel(
    hid, gain, w, cot, a1, a2, anc, mom,
    proj_out, m1_out, m2_out, anc_out, mom_out,
    hv, gv, wv, cotall, a1v, a2v, ancv, momv, scalev, nts, nta, gsc, pacc, sib, psend, precv, pout,
    ysend, yrecv, wrecv, zsend, zrecv, xown, xrecv, ancn, momn,
    load_sem, out_sem, cot_ss, cot_rs, x_ss, x_rs, w_ss, w_rs, y_ss, y_rs, z_ss, z_rs, xl_ss, xl_rs,
    sib_ss, sib_rs, p_ss, p_rs,
):
    r, f = lax.axis_index("rep"), lax.axis_index("fsdp")
    y, z, xl = lax.div(r, 16), lax.rem(lax.div(r, 2), NZ), lax.rem(r, 2)
    xh, c = lax.div(f, 2), lax.rem(f, 2)
    inv_root = 4096 ** (-0.5)

    peers = ((1 - xh) * 2 + c, (1 - xh) * 2 + 1 - c, xh * 2 + 1 - c)
    at_fsdp = [(r, p) for p in peers]
    ypeer = [None] + [lax.rem(y + d, NY) for d in range(1, NY)]
    at_y = [None] + [((ypeer[d] * NZ + z) * 2 + xl, f) for d in range(1, NY)]
    zpeer = [lax.rem(z + d, NZ) for d in DIST]
    at_z = [((y * NZ + p) * 2 + xl, f) for p in zpeer]
    at_xl = ((y * NZ + z) * 2 + 1 - xl, f)

    def remote(src, dst, ss, rs, to):
        return pltpu.make_async_remote_copy(
            src_ref=src, dst_ref=dst, send_sem=ss, recv_sem=rs, device_id=to, device_id_type=MESH
        )

    loads = {}
    for i, (name, src, dst) in enumerate((
        ("hid", hid, hv), ("gain", gain, gv), ("w", w, wv), ("cot", cot, cotall.at[:, f]),
        ("a1", a1, a1v), ("a2", a2, a2v), ("anc", anc, ancv), ("mom", mom, momv),
    )):
        loads[name] = pltpu.make_async_copy(src, dst, load_sem.at[i])
        loads[name].start()

    barrier = pltpu.get_barrier_semaphore()
    others = at_fsdp + at_y[1:] + at_z[:-1] + [at_xl]
    for to in others:
        pl.semaphore_signal(barrier, inc=1, device_id=to, device_id_type=MESH)
    pl.semaphore_wait(barrier, len(others))

    cot_p = remote(cot, cotall.at[:, f], cot_ss.at[0], cot_rs.at[0], at_fsdp[0])
    cot_s = remote(cot, cotall.at[:, f], cot_ss.at[1], cot_rs.at[1], at_fsdp[2])
    cot_p.start()
    cot_s.start()
    w_copies = []
    for d in range(1, NY):
        cp = remote(w.at[ypeer[d]], wrecv.at[y], w_ss.at[d], w_rs.at[d], at_y[d])
        cp.start()
        w_copies.append(cp)

    loads["hid"].wait()
    loads["gain"].wait()

    def squares(j, acc):
        wide = hv[:, pl.ds(pl.multiple_of(j * 128, 128), 128)].astype(F32)
        return acc + wide * wide

    acc = lax.fori_loop(0, 32, squares, jnp.zeros((256, 128), F32))
    mean = jnp.sum(acc, axis=1, keepdims=True) * (1.0 / 4096)
    scalev[...] = jnp.broadcast_to(lax.rsqrt(mean + 1e-05), (256, 128))

    for i, owner in enumerate((*peers, f)):

        def block(j, carry, i=i, owner=owner):
            cols = pl.ds(pl.multiple_of(owner * 1024 + j * 128, 128), 128)
            wide = hv[:, cols].astype(F32)
            normed = (wide * scalev[...] * gv[:, cols]).astype(BF)
            turned = normed.T
            yy, zz = lax.div(j, 2), lax.rem(j, 2) * 4
            for h in range(2):
                part = turned[:, h * 128 : (h + 1) * 128].reshape(4, 32, 128)
                if i < 3:
                    nts[i, h, yy, pl.ds(zz, 4)] = part
                else:
                    nta[h, f, yy, pl.ds(zz, 4)] = part
            return carry

        lax.fori_loop(0, 8, block, 0)

    groups = []
    for g in range(12):
        copies = []
        for p in range(3):
            if g < 4:
                src, dst = nts.at[p, 0, g], nta.at[0, f, g]
            else:
                src, dst = nts.at[p, 1, :, zpeer[g - 4]], nta.at[1, f, :, zpeer[g - 4]]
            copies.append(remote(src, dst, x_ss.at[g, p], x_rs.at[g, p], at_fsdp[p]))
        groups.append(copies)

    def start_group(g):
        if g < len(groups):
            for cp in groups[g]:
                cp.start()

    def take_group(g):
        for cp in groups[g]:
            cp.wait_recv()
        for cp in groups[g]:
            cp.wait_send()
        start_group(g + AHEAD)

    for g in range(AHEAD):
        start_group(g)

    loads["cot"].wait()
    loads["w"].wait()
    cot_p.wait_recv()
    passed = cotall.at[:, peers[0]]
    cot_f = remote(passed, passed, cot_ss.at[2], cot_rs.at[2], at_fsdp[2])
    cot_f.start()

    def put_partial(h, part, first):
        for s in range(4):
            piece = part[:, s * 128 : (s + 1) * 128]
            if first:
                pacc[h, s] = piece
            else:
                pacc[h, s] += piece

    sib_copies, p_copies = [], []

    def to_sibling(h):
        for q, owner in enumerate((peers[2], peers[1])):
            cp = remote(pacc.at[h, owner], sib.at[h, q], sib_ss.at[h, q], sib_rs.at[h, q], at_fsdp[2])
            cp.start()
            sib_copies.append(cp)

    def to_partner(h):
        sib_copies[2 * h + 1].wait_recv()
        psend[h] = (pacc[h, peers[0]] + sib[h, 1]).astype(BF)
        cp = remote(psend.at[h], precv.at[h], p_ss.at[h], p_rs.at[h], at_fsdp[0])
        cp.start()
        p_copies.append(cp)

    for g in range(4):
        take_group(g)
        tokens = jnp.concatenate([nta[0, s, g].reshape(256, 128) for s in range(4)], axis=1)
        put_partial(0, contract_first(wv[g].reshape(256, KV), tokens), g == 0)
    to_sibling(0)

    cot_s.wait_recv()
    cot_f.wait_recv()
    loads["a1"].wait()
    loads["a2"].wait()
    to_partner(0)

    y_copies, z_copies, outs = [], [], []

    def local_out(src, dst):
        cp = pltpu.make_async_copy(src, dst, out_sem.at[len(outs)])
        cp.start()
        outs.append(cp)

    def sum_y(k):
        for cp in y_copies[k]:
            cp.wait_recv()
        steps = ysend[k, y].astype(F32)
        weights = wv[y, zpeer[k]].astype(F32)
        for d in range(1, NY):
            steps += yrecv[k, ypeer[d]].astype(F32)
            weights += wrecv[ypeer[d], zpeer[k]].astype(F32)
        total = (1.0 - inner_rate * decay_rate) * weights - inner_rate * steps
        zsend[k] = total.reshape(2, 16, KV)
        if DIST[k]:
            cp = remote(zsend.at[k], zrecv.at[k], z_ss.at[k], z_rs.at[k], at_z[k])
            cp.start()
            z_copies.append(cp)

    def chunk_tokens(k):
        parts = [
            jnp.concatenate([nta[h, s, :, zpeer[k]].reshape(128, 128) for s in range(4)], axis=1)
            for h in range(2)
        ]
        return parts

    for k in range(8):
        take_group(4 + k)
        halves = chunk_tokens(k)
        grad = jnp.dot(halves[0], cotall[0].reshape(512, KV), preferred_element_type=F32)
        grad += jnp.dot(halves[1], cotall[1].reshape(512, KV), preferred_element_type=F32)
        gsc[...] = (grad * inv_root).reshape(4, 32, KV)
        for yy in range(4):
            g = gsc[yy]
            one = beta_one * a1v[yy, zpeer[k]] + (1.0 - beta_one) * g
            two = beta_two * a2v[yy, zpeer[k]] + (1.0 - beta_two) * g * g
            a1v[yy, zpeer[k]] = one
            a2v[yy, zpeer[k]] = two
            ysend[k, yy] = (one / (jnp.sqrt(two) + adam_eps)).astype(BF)
        copies = []
        for d in range(1, NY):
            cp = remote(ysend.at[k, ypeer[d]], yrecv.at[k, y], y_ss.at[k, d], y_rs.at[k, d], at_y[d])
            cp.start()
            copies.append(cp)
        y_copies.append(copies)
        local_out(a1v.at[:, zpeer[k]], m1_out.at[:, zpeer[k]])
        local_out(a2v.at[:, zpeer[k]], m2_out.at[:, zpeer[k]])
        if k % 2:
            tokens = jnp.concatenate([chunk_tokens(k - 1)[1], halves[1]], axis=0)
            weights = jnp.concatenate(
                [wv[:, zpeer[k - 1]].reshape(128, KV), wv[:, zpeer[k]].reshape(128, KV)], axis=0
            )
            put_partial(1, contract_first(weights, tokens), k == 1)
        if k == 7:
            to_sibling(1)
        if k == LAG:
            for cp in w_copies:
                cp.wait_recv()
        if k >= LAG:
            sum_y(k - LAG)

    to_partner(1)
    for k in range(8 - LAG, 8):
        sum_y(k)

    total = zsend[7]
    for cp, k in zip(z_copies, range(7)):
        cp.wait_recv()
        total += zrecv[k]
    xown[...] = total
    cp_xl = remote(xown.at[1 - xl], xrecv, xl_ss, xl_rs, at_xl)
    cp_xl.start()

    def finish(h):
        sib_copies[2 * h].wait_recv()
        p_copies[h].wait_recv()
        whole = (pacc[h, f] + sib[h, 0] + precv[h].astype(F32)) * inv_root
        pout[h] = whole.astype(BF).T
        local_out(pout.at[h], proj_out.at[h])

    finish(0)
    cp_xl.wait_recv()
    loads["anc"].wait()
    loads["mom"].wait()
    mean_delta = ancv[...] - (xown[xl] + xrecv[...]) * (1.0 / REPLICAS)
    new_momentum = nesterov_mu * momv[...] + mean_delta
    momn[...] = new_momentum
    ancn[...] = ancv[...] - outer_rate * (nesterov_mu * new_momentum + mean_delta)
    local_out(momn, mom_out)
    local_out(ancn, anc_out)
    finish(1)

    for cp in [cot_p, cot_s, cot_f, *w_copies, *sum(y_copies, []), *z_copies, *sib_copies, *p_copies, cp_xl]:
        cp.wait_send()
    for cp in outs:
        cp.wait()


def per_device(
    hidden_in, norm_gain, replica_weight, cotangent, adam_first, adam_second, anchor, outer_momentum
):
    any_space = pl.BlockSpec(memory_space=pl.ANY)
    dma = pltpu.SemaphoreType.DMA
    rows = (NY, NZ, 32)
    outs = pl.pallas_call(
        kernel,
        name="diloco_step",
        out_shape=(
            jax.ShapeDtypeStruct((2, 128, KV), BF),
            jax.ShapeDtypeStruct((*rows, KV), F32),
            jax.ShapeDtypeStruct((*rows, KV), F32),
            jax.ShapeDtypeStruct((16, KV), F32),
            jax.ShapeDtypeStruct((16, KV), F32),
        ),
        in_specs=[any_space] * 8,
        out_specs=[any_space] * 5,
        scratch_shapes=[
            pltpu.VMEM((256, 4096), BF),
            pltpu.VMEM((1, 4096), F32),
            pltpu.VMEM((*rows, KV), BF),
            pltpu.VMEM((2, 4, 128, KV), BF),
            pltpu.VMEM((*rows, KV), F32),
            pltpu.VMEM((*rows, KV), F32),
            pltpu.VMEM((16, KV), F32),
            pltpu.VMEM((16, KV), F32),
            pltpu.VMEM((256, 128), F32),
            pltpu.VMEM((3, 2, *rows, 128), BF),
            pltpu.VMEM((2, 4, *rows, 128), BF),
            pltpu.VMEM((4, 32, KV), F32),
            pltpu.VMEM((2, 4, KV, 128), F32),
            pltpu.VMEM((2, 2, KV, 128), F32),
            pltpu.VMEM((2, KV, 128), BF),
            pltpu.VMEM((2, KV, 128), BF),
            pltpu.VMEM((2, 128, KV), BF),
            pltpu.VMEM((8, NY, 32, KV), BF),
            pltpu.VMEM((8, NY, 32, KV), BF),
            pltpu.VMEM((NY, NZ, 32, KV), BF),
            pltpu.VMEM((8, 2, 16, KV), F32),
            pltpu.VMEM((8, 2, 16, KV), F32),
            pltpu.VMEM((2, 16, KV), F32),
            pltpu.VMEM((16, KV), F32),
            pltpu.VMEM((16, KV), F32),
            pltpu.VMEM((16, KV), F32),
            dma((8,)),
            dma((20,)),
            dma((3,)), dma((3,)),
            dma((12, 3)), dma((12, 3)),
            dma((NY,)), dma((NY,)),
            dma((8, NY)), dma((8, NY)),
            dma((8,)), dma((8,)),
            dma, dma,
            dma((2, 2)), dma((2, 2)),
            dma((2,)), dma((2,)),
        ],
        compiler_params=pltpu.CompilerParams(
            collective_id=0, has_side_effects=True, vmem_limit_bytes=56 << 20
        ),
        cost_estimate=pl.CostEstimate(
            flops=4 * 256 * 4096 * 512, bytes_accessed=12 << 20, transcendentals=1 << 20
        ),
    )(
        hidden_in.reshape(256, 4096),
        norm_gain.reshape(1, 4096),
        replica_weight.reshape(*rows, KV),
        cotangent.reshape(2, 128, KV),
        adam_first.reshape(*rows, KV),
        adam_second.reshape(*rows, KV),
        anchor,
        outer_momentum,
    )
    projected, first, second, new_anchor, new_momentum = outs
    return (
        projected.reshape(1, 256, KV),
        first.reshape(1, 1024, KV),
        second.reshape(1, 1024, KV),
        new_anchor,
        new_momentum,
    )


def solution(mesh):
    placed = (
        P("rep", "fsdp", None),
        P(),
        P("rep", "fsdp", None),
        P("rep", "fsdp", None),
        P("rep", "fsdp", None),
        P("rep", "fsdp", None),
        P(("fsdp", "rep"), None),
        P(("fsdp", "rep"), None),
    )
    return jax.shard_map(
        per_device,
        mesh=mesh,
        in_specs=placed,
        out_specs=(
            P("rep", "fsdp", None),
            P("rep", "fsdp", None),
            P("rep", "fsdp", None),
            P(("fsdp", "rep"), None),
            P(("fsdp", "rep"), None),
        ),
        check_vma=False,
    )
```

time: 991 us -> 65.6 us (0.07)
  waiting for transfers between devices: 957 us -> 0 us
  Pallas kernels: 0 us -> 57 us
  between operations: 15.3 us -> 0.65 us
    psum x1 -> x0, waiting for transfers between devices: 607 us -> none  [per_device(): summed = lax.psum(full_anchor - updated, 'rep')]
    all_gather x2 -> x0, waiting for transfers between devices: 348 us -> none  [the longest x1 315 us: per_device(): full_anchor = lax.all_gather(anchor, 'rep', axis=0, tiled=True)]
    pallas_call x0 -> x1, Pallas kernels: none -> 57 us  [per_device(): pl.pallas_call(kernel, name='diloco_step', out_shape=(jax.ShapeDtypeStruc...]
  transfers between devices with their start and end apart: 4 -> 0, of which waited for: 3 -> 0; matrix products, arithmetic and copies ran while one was open for 2% -> 0% of each run, Pallas kernels for 0% -> 0%
where the time goes in v1:
time: 65.6 us; the launch traced here: 65.1 us
  Pallas kernels  57 us (87%)
  local copies, waits for them, and re-layouts  7.46 us (11%)
    pallas_call x1, Pallas kernels, per_device(): pl.pallas_call(kernel, name='diloco_step', out_shape=(jax.ShapeDtypeStruc...  57 us
    unnamed x11, local copies, waits for them, and re-layouts  7.46 us

profile of v1, /device:TPU:2, one launch (start us, length us, event | category | flops | bytes accessed | tf_op | source)
XLA Modules:
  0.0 65.1 jit_solution(17741847059371580034)
XLA Ops:
  0.6 57.0 %diloco_step.1 = (bf16[2,128,512]{2,1,0:T(8,128)(2,1)}, f32[4,8,32,512]{3,2,1,0:T(8,128)}, f32[4,8,32,512]{3,2,1,0:T(8,128)}, f32[16,512]{1,0:T(8,128)}, f32[16,512]{1,0:T(8,128)}) custom-call(bf16[256,4096]{1,0:T(8,128)(2,1)} %bitcast.12, f32[1,4096]{1,0:T(1,128)} %bitcast.17, bf16[4,8,32,512]{3,2,1,0:T(8,128)(2,1)} %bitcast.15, ...), custom_call_target="tpu_custom_call" | custom-call | flops 2147483648 | bytes 12582912 | tf_op jit(solution)/shard_map/diloco_step/pallas_call | solution.py:284
  57.7 1.7 %copy.18 = bf16[1,256,512]{2,1,0:T(8,128)(2,1)} copy(bf16[1,256,512]{2,1,0:T(8,128)(2,1)} %bitcast.11) | data formatting | bytes 524288
  59.3 0.0 copy-start
  59.3 3.2 %copy.19 = f32[1,1024,512]{2,1,0:T(8,128)} copy(f32[1,1024,512]{2,1,0:T(8,128)} %bitcast.10) | data formatting | bytes 4194304
  62.6 0.0 copy-done
  62.6 0.0 copy-start.2
  62.6 0.0 copy-start.1
  62.6 1.3 %copy.20 = f32[1,1024,512]{2,1,0:T(8,128)} copy(f32[1,1024,512]{2,1,0:T(8,128)S(1)} %bitcast.9) | data formatting | bytes 4194304
  63.9 0.0 copy-done.2
  63.9 0.6 copy.21
  64.5 0.0 copy-done.1
  64.5 0.6 copy.22
Async XLA Ops:
  59.3 3.2 %copy-start = (f32[4,8,32,512]{3,2,1,0:T(8,128)S(1)}, f32[4,8,32,512]{3,2,1,0:T(8,128)}, u32[]{:S(2)}) copy-start(f32[4,8,32,512]{3,2,1,0:T(8,128)} %get-tuple-element.12) | copy-start | bytes 6291460
  62.6 1.3 %copy-start.2 = (f32[16,512]{1,0:T(8,128)S(1)}, f32[16,512]{1,0:T(8,128)}, u32[]{:S(2)}) copy-start(f32[16,512]{1,0:T(8,128)} %get-tuple-element.23) | copy-start | bytes 98308
  62.6 1.9 %copy-start.1 = (f32[16,512]{1,0:T(8,128)S(1)}, f32[16,512]{1,0:T(8,128)}, u32[]{:S(2)}) copy-start(f32[16,512]{1,0:T(8,128)} %get-tuple-element.24) | copy-start | bytes 98308

commit v2 on v1

v2 whole, which is shorter than its diff:
```python
import jax
import jax.numpy as jnp
from jax import lax
from jax.experimental import pallas as pl
from jax.experimental.pallas import tpu as pltpu
from jax.sharding import PartitionSpec as P

MESH = pl.DeviceIdType.MESH
BF, F32 = jnp.bfloat16, jnp.float32

beta_one = 0.9
beta_two = 0.95
adam_eps = 1e-08
inner_rate = 0.02
decay_rate = 0.1
nesterov_mu = 0.9
outer_rate = 0.7

NY, NZ, REPLICAS = 4, 8, 64
DIST = (4, 3, 5, 2, 6, 1, 7, 0)
AHEAD = 3
LAG = 2
KV = 512
PIECES = 2
PK = KV // PIECES


def contract_first(a, b):
    return lax.dot_general(a, b, (((0,), (0,)), ((), ())), preferred_element_type=F32)


def kernel(
    hid, gain, w, cot, a1, a2, anc, mom,
    pout, m1v, m2v, ancn, momn,
    hv, gv, wv, cotall, a1v, a2v, ancv, momv, scalev, nts, nta, gsc, pacc, sib, psend, precv,
    ysend, yrecv, wrecv, zsend, zrecv, xown, xrecv,
    load_sem, cot_ss, cot_rs, x_ss, x_rs, w_ss, w_rs, y_ss, y_rs, z_ss, z_rs, xl_ss, xl_rs,
    sib_ss, sib_rs, p_ss, p_rs,
):
    r, f = lax.axis_index("rep"), lax.axis_index("fsdp")
    y, z, xl = lax.div(r, 16), lax.rem(lax.div(r, 2), NZ), lax.rem(r, 2)
    xh, c = lax.div(f, 2), lax.rem(f, 2)
    inv_root = 4096 ** (-0.5)

    peers = ((1 - xh) * 2 + c, (1 - xh) * 2 + 1 - c, xh * 2 + 1 - c)
    at_fsdp = [(r, p) for p in peers]
    ypeer = [None] + [lax.rem(y + d, NY) for d in range(1, NY)]
    at_y = [None] + [((ypeer[d] * NZ + z) * 2 + xl, f) for d in range(1, NY)]
    at_z = [((y * NZ + lax.rem(z + d, NZ)) * 2 + xl, f) for d in DIST]

    def owner_z(k):
        return lax.rem(z + 4 + lax.div(k + 1, 2) * (1 - 2 * lax.rem(k, 2)), NZ)

    at_xl = ((y * NZ + z) * 2 + 1 - xl, f)

    def remote(src, dst, ss, rs, to):
        return pltpu.make_async_remote_copy(
            src_ref=src, dst_ref=dst, send_sem=ss, recv_sem=rs, device_id=to, device_id_type=MESH
        )

    barrier = pltpu.get_barrier_semaphore()
    others = at_fsdp + at_y[1:] + at_z[:-1] + [at_xl]
    for to in others:
        pl.semaphore_signal(barrier, inc=1, device_id=to, device_id_type=MESH)

    loads = {}
    for i, (name, src, dst) in enumerate((
        ("hid", hid, hv), ("gain", gain, gv), ("w", w, wv), ("cot", cot, cotall.at[:, f]),
        ("a1", a1, a1v), ("a2", a2, a2v), ("anc", anc, ancv), ("mom", mom, momv),
    )):
        loads[name] = pltpu.make_async_copy(src, dst, load_sem.at[i])
        loads[name].start()

    pl.semaphore_wait(barrier, len(others))

    cot_p = remote(cot, cotall.at[:, f], cot_ss.at[0], cot_rs.at[0], at_fsdp[0])
    cot_s = remote(cot, cotall.at[:, f], cot_ss.at[1], cot_rs.at[1], at_fsdp[2])
    cot_p.start()
    cot_s.start()
    w_copies = []
    for d in range(1, NY):
        cp = remote(w.at[ypeer[d]], wrecv.at[y], w_ss.at[d], w_rs.at[d], at_y[d])
        cp.start()
        w_copies.append(cp)

    loads["hid"].wait()
    loads["gain"].wait()

    def squares(j, acc):
        wide = hv[:, pl.ds(pl.multiple_of(j * 128, 128), 128)].astype(F32)
        return acc + wide * wide

    acc = lax.fori_loop(0, 32, squares, jnp.zeros((256, 128), F32))
    mean = jnp.sum(acc, axis=1, keepdims=True) * (1.0 / 4096)
    scalev[...] = jnp.broadcast_to(lax.rsqrt(mean + 1e-05), (256, 128))

    def turn(owner, j):
        cols = pl.ds(pl.multiple_of(owner * 1024 + j * 128, 128), 128)
        wide = hv[:, cols].astype(F32)
        turned = (wide * scalev[...] * gv[:, cols]).astype(BF).T
        return [turned[:, h * 128 : (h + 1) * 128].reshape(4, 32, 128) for h in range(2)]

    def block_for_peer(n, carry):
        i, j = lax.div(n, 8), lax.rem(n, 8)
        up, side = lax.div(i, 2), lax.div(i + 1, 2)
        owner = ((1 - xh) * (1 - up) + xh * up) * 2 + c * (1 - side) + (1 - c) * side
        for h, part in enumerate(turn(owner, j)):
            nts[i, h, lax.div(j, 2), pl.ds(lax.rem(j, 2) * 4, 4)] = part
        return carry

    def block_for_me(j, carry):
        for h, part in enumerate(turn(f, j)):
            nta[h, f, lax.div(j, 2), pl.ds(lax.rem(j, 2) * 4, 4)] = part
        return carry

    lax.fori_loop(0, 24, block_for_peer, 0)

    def x_copy(k, h, p):
        zz = owner_z(k)
        return remote(nts.at[p, h, :, zz], nta.at[h, f, :, zz], x_ss.at[k, h, p], x_rs.at[k, h, p], at_fsdp[p])

    def start_group(g):
        late = lax.div(g, 6)
        for n in range(2):
            k, h = g * (1 - late) + (6 + n) * late, n * (1 - late) + (g - 6) * late
            for p in range(3):
                x_copy(k, h, p).start()

    def take(k, h):
        for p in range(3):
            x_copy(k, h, p).wait_recv()

    def start_first(g, carry):
        start_group(g)
        return carry

    lax.fori_loop(0, AHEAD, start_first, 0)
    lax.fori_loop(0, 8, block_for_me, 0)
    pacc[...] = jnp.zeros_like(pacc)

    loads["cot"].wait()
    loads["w"].wait()
    cot_p.wait_recv()
    passed = cotall.at[:, peers[0]]
    cot_f = remote(passed, passed, cot_ss.at[2], cot_rs.at[2], at_fsdp[2])
    cot_f.start()

    def sib_copy(h, q, i):
        rows = pl.ds(i * PK, PK)
        owner = (peers[2], peers[1])[q]
        return remote(
            pacc.at[h, owner, rows], sib.at[h, q, rows], sib_ss.at[h, q, i], sib_rs.at[h, q, i], at_fsdp[2]
        )

    def p_copy(h, i):
        rows = pl.ds(i * PK, PK)
        return remote(psend.at[h, rows], precv.at[h, rows], p_ss.at[h, i], p_rs.at[h, i], at_fsdp[0])

    def to_partner(h):
        def piece(i, carry):
            rows = pl.ds(i * PK, PK)
            sib_copy(h, 1, i).wait_recv()
            psend[h, rows] = (pacc[h, peers[0], rows] + sib[h, 1, rows]).astype(BF)
            p_copy(h, i).start()
            return carry

        lax.fori_loop(0, PIECES, piece, 0)

    def chunk_tokens(k, h):
        zz = owner_z(k)
        return jnp.concatenate([nta[h, s, :, zz].reshape(128, 128) for s in range(4)], axis=1)

    def pair_partial(k, h, rows, n):
        tokens = jnp.concatenate([chunk_tokens(k - 1, h), chunk_tokens(k, h)], axis=0)
        weights = jnp.concatenate([wv[:, owner_z(j), :, rows].reshape(128, n) for j in (k - 1, k)], axis=0)
        part = contract_first(weights, tokens)
        for s in range(4):
            pacc[h, s, rows] += part[:, s * 128 : (s + 1) * 128]

    def last_partial(h):
        def piece(i, carry):
            pair_partial(7, h, pl.ds(pl.multiple_of(i * PK, PK), PK), PK)
            sib_copy(h, 1, i).start()
            sib_copy(h, 0, i).start()
            return carry

        lax.fori_loop(0, PIECES, piece, 0)

    cot_s.wait_recv()
    cot_f.wait_recv()
    loads["a1"].wait()
    loads["a2"].wait()

    def y_copy(k, d):
        return remote(ysend.at[k, ypeer[d]], yrecv.at[k, y], y_ss.at[k, d], y_rs.at[k, d], at_y[d])

    def z_copy(k):
        to = ((y * NZ + owner_z(k)) * 2 + xl, f)
        return remote(zsend.at[k], zrecv.at[k], z_ss.at[k], z_rs.at[k], to)

    def sum_y(k, own=False):
        for d in range(1, NY):
            y_copy(k, d).wait_recv()
        zz = owner_z(k)
        steps = ysend[k, y].astype(F32)
        weights = wv[y, zz].astype(F32)
        for d in range(1, NY):
            steps += yrecv[k, ypeer[d]].astype(F32)
            weights += wrecv[ypeer[d], zz].astype(F32)
        total = (1.0 - inner_rate * decay_rate) * weights - inner_rate * steps
        zsend[k] = total.reshape(2, 16, KV)
        if not own:
            z_copy(k).start()

    def inner_step(k):
        zz = owner_z(k)
        grad = jnp.dot(chunk_tokens(k, 0), cotall[0].reshape(512, KV), preferred_element_type=F32)
        grad += jnp.dot(chunk_tokens(k, 1), cotall[1].reshape(512, KV), preferred_element_type=F32)
        gsc[...] = (grad * inv_root).reshape(4, 32, KV)

        def rows(yy, carry):
            g = gsc[yy]
            one = beta_one * a1v[yy, zz] + (1.0 - beta_one) * g
            two = beta_two * a2v[yy, zz] + (1.0 - beta_two) * g * g
            m1v[yy, zz] = one
            m2v[yy, zz] = two
            ysend[k, yy] = (one / (jnp.sqrt(two) + adam_eps)).astype(BF)
            return carry

        lax.fori_loop(0, 4, rows, 0)
        for d in range(1, NY):
            y_copy(k, d).start()

    def early(k, carry):
        take(k, 0)
        take(k, 1)

        @pl.when(k + AHEAD < 8)
        def _():
            start_group(k + AHEAD)

        inner_step(k)

        @pl.when(k == LAG)
        def _():
            for cp in w_copies:
                cp.wait_recv()

        @pl.when(k >= LAG)
        def _():
            sum_y(k - LAG)

        @pl.when(lax.rem(k, 2) == 1)
        def _():
            def half(h, inner):
                pair_partial(k, h, slice(None), KV)
                return inner

            lax.fori_loop(0, 2, half, 0)

        return carry

    lax.fori_loop(0, 6, early, 0)
    take(6, 0)
    take(7, 0)
    last_partial(0)

    def late(k, carry):
        take(k, 1)

        @pl.when(k == 7)
        def _():
            to_partner(0)

        inner_step(k)
        sum_y(k - LAG)
        return carry

    lax.fori_loop(6, 8, late, 0)
    last_partial(1)
    sum_y(6)
    to_partner(1)
    sum_y(7, own=True)

    def add_z(k, total):
        z_copy(k).wait_recv()
        return total + zrecv[k]

    total = lax.fori_loop(0, 7, add_z, zsend[7])
    xown[...] = total
    cp_xl = remote(xown.at[1 - xl], xrecv, xl_ss, xl_rs, at_xl)
    cp_xl.start()

    def finish(h):
        def piece(i, carry):
            rows = pl.ds(pl.multiple_of(i * PK, PK), PK)
            sib_copy(h, 0, i).wait_recv()
            p_copy(h, i).wait_recv()
            whole = (pacc[h, f, rows] + sib[h, 0, rows] + precv[h, rows].astype(F32)) * inv_root
            pout[h, :, rows] = whole.astype(BF).T
            return carry

        lax.fori_loop(0, PIECES, piece, 0)

    finish(0)
    cp_xl.wait_recv()
    loads["anc"].wait()
    loads["mom"].wait()
    mean_delta = ancv[...] - (xown[xl] + xrecv[...]) * (1.0 / REPLICAS)
    new_momentum = nesterov_mu * momv[...] + mean_delta
    momn[...] = new_momentum
    ancn[...] = ancv[...] - outer_rate * (nesterov_mu * new_momentum + mean_delta)
    finish(1)

    for cp in [cot_p, cot_s, cot_f, *w_copies, cp_xl]:
        cp.wait_send()

    def sent(k, carry):
        for h in range(2):
            for p in range(3):
                x_copy(k, h, p).wait_send()
        for d in range(1, NY):
            y_copy(k, d).wait_send()

        @pl.when(k < 7)
        def _():
            z_copy(k).wait_send()

        return carry

    lax.fori_loop(0, 8, sent, 0)
    for h in range(2):
        for i in range(PIECES):
            for q in range(2):
                sib_copy(h, q, i).wait_send()
            p_copy(h, i).wait_send()


def write_out(*refs):
    copies = [pltpu.make_async_copy(refs[i], refs[5 + i], refs[10].at[i]) for i in range(5)]
    for cp in copies:
        cp.start()
    for cp in copies:
        cp.wait()


def per_device(
    hidden_in, norm_gain, replica_weight, cotangent, adam_first, adam_second, anchor, outer_momentum
):
    any_space = pl.BlockSpec(memory_space=pl.ANY)
    dma = pltpu.SemaphoreType.DMA
    in_vmem = pl.BlockSpec(memory_space=pltpu.VMEM)
    rows = (NY, NZ, 32)
    results = [((2, 128, KV), BF), ((*rows, KV), F32), ((*rows, KV), F32), ((16, KV), F32), ((16, KV), F32)]
    outs = pl.pallas_call(
        kernel,
        name="diloco_step",
        out_shape=tuple(pltpu.VMEM(*o) for o in results),
        in_specs=[any_space] * 8,
        out_specs=[in_vmem] * 5,
        scratch_shapes=[
            pltpu.VMEM((256, 4096), BF),
            pltpu.VMEM((1, 4096), F32),
            pltpu.VMEM((*rows, KV), BF),
            pltpu.VMEM((2, 4, 128, KV), BF),
            pltpu.VMEM((*rows, KV), F32),
            pltpu.VMEM((*rows, KV), F32),
            pltpu.VMEM((16, KV), F32),
            pltpu.VMEM((16, KV), F32),
            pltpu.VMEM((256, 128), F32),
            pltpu.VMEM((3, 2, *rows, 128), BF),
            pltpu.VMEM((2, 4, *rows, 128), BF),
            pltpu.VMEM((4, 32, KV), F32),
            pltpu.VMEM((2, 4, KV, 128), F32),
            pltpu.VMEM((2, 2, KV, 128), F32),
            pltpu.VMEM((2, KV, 128), BF),
            pltpu.VMEM((2, KV, 128), BF),
            pltpu.VMEM((8, NY, 32, KV), BF),
            pltpu.VMEM((8, NY, 32, KV), BF),
            pltpu.VMEM((NY, NZ, 32, KV), BF),
            pltpu.VMEM((8, 2, 16, KV), F32),
            pltpu.VMEM((8, 2, 16, KV), F32),
            pltpu.VMEM((2, 16, KV), F32),
            pltpu.VMEM((16, KV), F32),
            dma((8,)),
            dma((3,)), dma((3,)),
            dma((8, 2, 3)), dma((8, 2, 3)),
            dma((NY,)), dma((NY,)),
            dma((8, NY)), dma((8, NY)),
            dma((8,)), dma((8,)),
            dma, dma,
            dma((2, 2, PIECES)), dma((2, 2, PIECES)),
            dma((2, PIECES)), dma((2, PIECES)),
        ],
        compiler_params=pltpu.CompilerParams(
            collective_id=0, has_side_effects=True, vmem_limit_bytes=52 << 20
        ),
        cost_estimate=pl.CostEstimate(
            flops=4 * 256 * 4096 * 512, bytes_accessed=12 << 20, transcendentals=1 << 20
        ),
    )(
        hidden_in.reshape(256, 4096),
        norm_gain.reshape(1, 4096),
        replica_weight.reshape(*rows, KV),
        cotangent.reshape(2, 128, KV),
        adam_first.reshape(*rows, KV),
        adam_second.reshape(*rows, KV),
        anchor,
        outer_momentum,
    )
    projected, first, second, new_anchor, new_momentum = pl.pallas_call(
        write_out,
        name="write_out",
        out_shape=tuple(jax.ShapeDtypeStruct(*o) for o in results),
        in_specs=[in_vmem] * 5,
        out_specs=[any_space] * 5,
        scratch_shapes=[dma((5,))],
        compiler_params=pltpu.CompilerParams(vmem_limit_bytes=1 << 20),
        cost_estimate=pl.CostEstimate(flops=0, bytes_accessed=5 << 20, transcendentals=0),
    )(*(pltpu.with_memory_space_constraint(o, pltpu.VMEM) for o in outs))
    return (
        projected.reshape(1, 256, KV),
        first.reshape(1, 1024, KV),
        second.reshape(1, 1024, KV),
        new_anchor,
        new_momentum,
    )


def solution(mesh):
    placed = (
        P("rep", "fsdp", None),
        P(),
        P("rep", "fsdp", None),
        P("rep", "fsdp", None),
        P("rep", "fsdp", None),
        P("rep", "fsdp", None),
        P(("fsdp", "rep"), None),
        P(("fsdp", "rep"), None),
    )
    return jax.shard_map(
        per_device,
        mesh=mesh,
        in_specs=placed,
        out_specs=(
            P("rep", "fsdp", None),
            P("rep", "fsdp", None),
            P("rep", "fsdp", None),
            P(("fsdp", "rep"), None),
            P(("fsdp", "rep"), None),
        ),
        check_vma=False,
    )
```

time: 65.6 us -> 55.7 us (0.85)
  local copies, waits for them, and re-layouts: 7.46 us -> 0 us
  Pallas kernels: 57 us -> 55 us
    unnamed x11 -> x0, local copies, waits for them, and re-layouts: 7.46 us -> none
    pallas_call x1 -> x2, Pallas kernels: 57 us -> 55 us  [the longest x1 52.8 us: per_device(): pl.pallas_call(kernel, name='diloco_step', out_shape=tuple((pltpu.VMEM(*o...]
where the time goes in v2:
time: 55.7 us; the launch traced here: 55.6 us
  Pallas kernels  55 us (99%)
  between operations  0.64 us (1%)
    pallas_call x1, Pallas kernels, per_device(): pl.pallas_call(kernel, name='diloco_step', out_shape=tuple((pltpu.VMEM(*o...  52.8 us
    pallas_call x1, Pallas kernels, per_device(): pl.pallas_call(write_out, name='write_out', out_shape=tuple((jax.ShapeDty...  2.15 us

profile of v2, /device:TPU:2, one launch (start us, length us, event | category | flops | bytes accessed | tf_op | source)
XLA Modules:
  0.0 55.6 jit_solution(12491568182275749286)
XLA Ops:
  0.6 52.8 %diloco_step.1 = (bf16[2,128,512]{2,1,0:T(8,128)(2,1)S(1)}, f32[4,8,32,512]{3,2,1,0:T(8,128)S(1)}, f32[4,8,32,512]{3,2,1,0:T(8,128)S(1)}, f32[16,512]{1,0:T(8,128)S(1)}, f32[16,512]{1,0:T(8,128)S(1)}) custom-call(bf16[256,4096]{1,0:T(8,128)(2,1)} %bitcast.9, f32[1,4096]{1,0:T(1,128)} %bitcast.17, bf16[4,8,32,512]{3,2,1,0:T(8,128)(2,1)} %bitcast.14, ...), custom_call_target="tpu_custom_call" | custom-call | flops 2147483648 | bytes 12582912 | tf_op jit(solution)/shard_map/diloco_step/pallas_call | solution.py:355
  53.5 2.1 %write_out.1 = (bf16[2,128,512]{2,1,0:T(8,128)(2,1)}, f32[4,8,32,512]{3,2,1,0:T(8,128)}, f32[4,8,32,512]{3,2,1,0:T(8,128)}, f32[16,512]{1,0:T(8,128)}, f32[16,512]{1,0:T(8,128)}) custom-call(bf16[2,128,512]{2,1,0:T(8,128)(2,1)S(1)} %get-tuple-element.15.refs_0_, f32[4,8,32,512]{3,2,1,0:T(8,128)S(1)} %get-tuple-element.16.refs_1_, ...), custom_call_target="tpu_custom_call" | custom-call | bytes 5242880 | tf_op jit(solution)/shard_map/write_out/pallas_call | solution.py:411

commit v3 on v2

--- a/solution.py
+++ b/solution.py
@@ -33,8 +33,8 @@
     hid, gain, w, cot, a1, a2, anc, mom,
     pout, m1v, m2v, ancn, momn,
     hv, gv, wv, cotall, a1v, a2v, ancv, momv, scalev, nts, nta, gsc, pacc, sib, psend, precv,
-    ysend, yrecv, wrecv, zsend, zrecv, xown, xrecv,
-    load_sem, cot_ss, cot_rs, x_ss, x_rs, w_ss, w_rs, y_ss, y_rs, z_ss, z_rs, xl_ss, xl_rs,
+    ysend, yrecv, ylast, wrecv, zsend, zrecv, xown, xrecv,
+    load_sem, cot_ss, cot_rs, x_ss, x_rs, w_ss, w_rs, y_ss, y_rs, yl_ss, yl_rs, z_ss, z_rs, xl_ss, xl_rs,
     sib_ss, sib_rs, p_ss, p_rs,
 ):
     r, f = lax.axis_index("rep"), lax.axis_index("fsdp")
@@ -51,7 +51,14 @@
     def owner_z(k):
         return lax.rem(z + 4 + lax.div(k + 1, 2) * (1 - 2 * lax.rem(k, 2)), NZ)
 
-    at_xl = ((y * NZ + z) * 2 + 1 - xl, f)
+    both_xl = (xl, 1 - xl)
+    last_to = [(d, e) for d in range(NY) for e in range(2) if d + e]
+    yring = [y] + ypeer[1:]
+
+    def at_last(d, e):
+        return ((yring[d] * NZ + z) * 2 + both_xl[e], f)
+
+    at_xl = at_last(0, 1)
 
     def remote(src, dst, ss, rs, to):
         return pltpu.make_async_remote_copy(
@@ -59,9 +66,12 @@
         )
 
     barrier = pltpu.get_barrier_semaphore()
-    others = at_fsdp + at_y[1:] + at_z[:-1] + [at_xl]
+    others = at_fsdp + at_z[:-1] + [at_last(*t) for t in last_to]
     for to in others:
         pl.semaphore_signal(barrier, inc=1, device_id=to, device_id_type=MESH)
+
+    def arrived(region, sem):
+        pltpu.make_async_copy(region, region, sem).wait()
 
     loads = {}
     for i, (name, src, dst) in enumerate((
@@ -69,7 +79,8 @@
         ("a1", a1, a1v), ("a2", a2, a2v), ("anc", anc, ancv), ("mom", mom, momv),
     )):
         loads[name] = pltpu.make_async_copy(src, dst, load_sem.at[i])
-        loads[name].start()
+        if name not in ("a1", "a2", "anc", "mom"):
+            loads[name].start()
 
     pl.semaphore_wait(barrier, len(others))
 
@@ -77,14 +88,14 @@
     cot_s = remote(cot, cotall.at[:, f], cot_ss.at[1], cot_rs.at[1], at_fsdp[2])
     cot_p.start()
     cot_s.start()
-    w_copies = []
     for d in range(1, NY):
-        cp = remote(w.at[ypeer[d]], wrecv.at[y], w_ss.at[d], w_rs.at[d], at_y[d])
+        cp = remote(w.at[ypeer[d]], wrecv.at[y], w_ss, w_rs, at_y[d])
         cp.start()
-        w_copies.append(cp)
 
     loads["hid"].wait()
     loads["gain"].wait()
+    for name in ("a1", "a2", "anc", "mom"):
+        loads[name].start()
 
     def squares(j, acc):
         wide = hv[:, pl.ds(pl.multiple_of(j * 128, 128), 128)].astype(F32)
@@ -115,23 +126,23 @@
 
     lax.fori_loop(0, 24, block_for_peer, 0)
 
-    def x_copy(k, h, p):
+    def start(k):
         zz = owner_z(k)
-        return remote(nts.at[p, h, :, zz], nta.at[h, f, :, zz], x_ss.at[k, h, p], x_rs.at[k, h, p], at_fsdp[p])
-
-    def start_group(g):
-        late = lax.div(g, 6)
-        for n in range(2):
-            k, h = g * (1 - late) + (6 + n) * late, n * (1 - late) + (g - 6) * late
-            for p in range(3):
-                x_copy(k, h, p).start()
-
-    def take(k, h):
         for p in range(3):
-            x_copy(k, h, p).wait_recv()
-
-    def start_first(g, carry):
-        start_group(g)
+            remote(nts.at[p, :, :, zz], nta.at[:, f, :, zz], x_ss, x_rs.at[k], at_fsdp[p]).start()
+
+    def start_half(h):
+        for p in range(3):
+            remote(nts.at[p, h, :, z], nta.at[h, f, :, z], x_ss, x_rs.at[7 + h], at_fsdp[p]).start()
+
+    def take(k):
+        arrived(nts.at[:, :, :, 0], x_rs.at[k])
+
+    def take_half(h):
+        arrived(nts.at[:, h, :, 0], x_rs.at[7 + h])
+
+    def start_first(k, carry):
+        start(k)
         return carry
 
     lax.fori_loop(0, AHEAD, start_first, 0)
@@ -149,12 +160,12 @@
         rows = pl.ds(i * PK, PK)
         owner = (peers[2], peers[1])[q]
         return remote(
-            pacc.at[h, owner, rows], sib.at[h, q, rows], sib_ss.at[h, q, i], sib_rs.at[h, q, i], at_fsdp[2]
+            pacc.at[h, owner, rows], sib.at[h, q, rows], sib_ss, sib_rs.at[h, q, i], at_fsdp[2]
         )
 
     def p_copy(h, i):
         rows = pl.ds(i * PK, PK)
-        return remote(psend.at[h, rows], precv.at[h, rows], p_ss.at[h, i], p_rs.at[h, i], at_fsdp[0])
+        return remote(psend.at[h, rows], precv.at[h, rows], p_ss, p_rs.at[h, i], at_fsdp[0])
 
     def to_partner(h):
         def piece(i, carry):
@@ -192,27 +203,31 @@
     loads["a2"].wait()
 
     def y_copy(k, d):
-        return remote(ysend.at[k, ypeer[d]], yrecv.at[k, y], y_ss.at[k, d], y_rs.at[k, d], at_y[d])
+        return remote(ysend.at[k, ypeer[d]], yrecv.at[k, y], y_ss, y_rs.at[k], at_y[d])
 
     def z_copy(k):
         to = ((y * NZ + owner_z(k)) * 2 + xl, f)
-        return remote(zsend.at[k], zrecv.at[k], z_ss.at[k], z_rs.at[k], to)
-
-    def sum_y(k, own=False):
-        for d in range(1, NY):
-            y_copy(k, d).wait_recv()
-        zz = owner_z(k)
-        steps = ysend[k, y].astype(F32)
+        return remote(zsend.at[k], zrecv.at[k], z_ss, z_rs, to)
+
+    def yl_copy(d, e):
+        src = ysend.at[7, yring[d], both_xl[e]]
+        return remote(src, ylast.at[y, xl], yl_ss, yl_rs, at_last(d, e))
+
+    def sum_weights(zz):
         weights = wv[y, zz].astype(F32)
         for d in range(1, NY):
+            weights += wrecv[ypeer[d], zz].astype(F32)
+        return (1.0 - inner_rate * decay_rate) * weights.reshape(2, 16, KV)
+
+    def sum_y(k):
+        arrived(yrecv.at[k, 0:3], y_rs.at[k])
+        steps = ysend[k, y].astype(F32)
+        for d in range(1, NY):
             steps += yrecv[k, ypeer[d]].astype(F32)
-            weights += wrecv[ypeer[d], zz].astype(F32)
-        total = (1.0 - inner_rate * decay_rate) * weights - inner_rate * steps
-        zsend[k] = total.reshape(2, 16, KV)
-        if not own:
-            z_copy(k).start()
-
-    def inner_step(k):
+        zsend[k] = sum_weights(owner_z(k)) - inner_rate * steps
+        z_copy(k).start()
+
+    def inner_step(k, last=False):
         zz = owner_z(k)
         grad = jnp.dot(chunk_tokens(k, 0), cotall[0].reshape(512, KV), preferred_element_type=F32)
         grad += jnp.dot(chunk_tokens(k, 1), cotall[1].reshape(512, KV), preferred_element_type=F32)
@@ -224,27 +239,31 @@
             two = beta_two * a2v[yy, zz] + (1.0 - beta_two) * g * g
             m1v[yy, zz] = one
             m2v[yy, zz] = two
-            ysend[k, yy] = (one / (jnp.sqrt(two) + adam_eps)).astype(BF)
+            ysend[k, yy] = (one / (jnp.sqrt(two) + adam_eps)).astype(BF).reshape(2, 16, KV)
             return carry
 
         lax.fori_loop(0, 4, rows, 0)
-        for d in range(1, NY):
-            y_copy(k, d).start()
+        for copy in [yl_copy(*t) for t in last_to] if last else [y_copy(k, d) for d in range(1, NY)]:
+            copy.start()
 
     def early(k, carry):
-        take(k, 0)
-        take(k, 1)
-
-        @pl.when(k + AHEAD < 8)
+        take(k)
+
+        @pl.when(k + AHEAD < 7)
         def _():
-            start_group(k + AHEAD)
+            start(k + AHEAD)
+
+        for h in range(2):
+
+            @pl.when(k + AHEAD == 7 + h)
+            def _(h=h):
+                start_half(h)
 
         inner_step(k)
 
         @pl.when(k == LAG)
         def _():
-            for cp in w_copies:
-                cp.wait_recv()
+            arrived(wv.at[0:3], w_rs)
 
         @pl.when(k >= LAG)
         def _():
@@ -260,33 +279,23 @@
 
         return carry
 
-    lax.fori_loop(0, 6, early, 0)
-    take(6, 0)
-    take(7, 0)
+    lax.fori_loop(0, 7, early, 0)
+    take_half(0)
     last_partial(0)
-
-    def late(k, carry):
-        take(k, 1)
-
-        @pl.when(k == 7)
-        def _():
-            to_partner(0)
-
-        inner_step(k)
-        sum_y(k - LAG)
-        return carry
-
-    lax.fori_loop(6, 8, late, 0)
+    sum_y(5)
+    take_half(1)
+    to_partner(0)
+    inner_step(7, last=True)
     last_partial(1)
     sum_y(6)
     to_partner(1)
-    sum_y(7, own=True)
 
     def add_z(k, total):
-        z_copy(k).wait_recv()
         return total + zrecv[k]
 
-    total = lax.fori_loop(0, 7, add_z, zsend[7])
+    arrived(zrecv, z_rs)
+
+    total = lax.fori_loop(0, 7, add_z, sum_weights(z))
     xown[...] = total
     cp_xl = remote(xown.at[1 - xl], xrecv, xl_ss, xl_rs, at_xl)
     cp_xl.start()
@@ -306,34 +315,25 @@
     cp_xl.wait_recv()
     loads["anc"].wait()
     loads["mom"].wait()
-    mean_delta = ancv[...] - (xown[xl] + xrecv[...]) * (1.0 / REPLICAS)
+    steps = ysend[7, y, xl].astype(F32)
+    arrived(ysend.at[0:7, 0, 0], yl_rs)
+    for d, e in last_to:
+        steps += ylast[yring[d], both_xl[e]].astype(F32)
+    mean_delta = ancv[...] - (xown[xl] + xrecv[...] - inner_rate * steps) * (1.0 / REPLICAS)
     new_momentum = nesterov_mu * momv[...] + mean_delta
     momn[...] = new_momentum
     ancn[...] = ancv[...] - outer_rate * (nesterov_mu * new_momentum + mean_delta)
     finish(1)
 
-    for cp in [cot_p, cot_s, cot_f, *w_copies, cp_xl]:
+    for cp in [cot_p, cot_s, cot_f, cp_xl]:
         cp.wait_send()
-
-    def sent(k, carry):
-        for h in range(2):
-            for p in range(3):
-                x_copy(k, h, p).wait_send()
-        for d in range(1, NY):
-            y_copy(k, d).wait_send()
-
-        @pl.when(k < 7)
-        def _():
-            z_copy(k).wait_send()
-
-        return carry
-
-    lax.fori_loop(0, 8, sent, 0)
-    for h in range(2):
-        for i in range(PIECES):
-            for q in range(2):
-                sib_copy(h, q, i).wait_send()
-            p_copy(h, i).wait_send()
+    arrived(wv.at[0:3], w_ss)
+    arrived(nts, x_ss)
+    arrived(yrecv.at[:, 0:3], y_ss)
+    arrived(ysend.at[0:7, 0, 0], yl_ss)
+    arrived(zsend, z_ss)
+    arrived(sib, sib_ss)
+    arrived(psend, p_ss)
 
 
 def write_out(*refs):
@@ -375,22 +375,24 @@
             pltpu.VMEM((2, 2, KV, 128), F32),
             pltpu.VMEM((2, KV, 128), BF),
             pltpu.VMEM((2, KV, 128), BF),
-            pltpu.VMEM((8, NY, 32, KV), BF),
-            pltpu.VMEM((8, NY, 32, KV), BF),
+            pltpu.VMEM((8, NY, 2, 16, KV), BF),
+            pltpu.VMEM((7, NY, 2, 16, KV), BF),
+            pltpu.VMEM((NY, 2, 16, KV), BF),
             pltpu.VMEM((NY, NZ, 32, KV), BF),
-            pltpu.VMEM((8, 2, 16, KV), F32),
-            pltpu.VMEM((8, 2, 16, KV), F32),
+            pltpu.VMEM((7, 2, 16, KV), F32),
+            pltpu.VMEM((7, 2, 16, KV), F32),
             pltpu.VMEM((2, 16, KV), F32),
             pltpu.VMEM((16, KV), F32),
             dma((8,)),
             dma((3,)), dma((3,)),
-            dma((8, 2, 3)), dma((8, 2, 3)),
-            dma((NY,)), dma((NY,)),
-            dma((8, NY)), dma((8, NY)),
-            dma((8,)), dma((8,)),
+            dma, dma((9,)),
             dma, dma,
-            dma((2, 2, PIECES)), dma((2, 2, PIECES)),
-            dma((2, PIECES)), dma((2, PIECES)),
+            dma, dma((7,)),
+            dma, dma,
+            dma, dma,
+            dma, dma,
+            dma, dma((2, 2, PIECES)),
+            dma, dma((2, PIECES)),
         ],
         compiler_params=pltpu.CompilerParams(
             collective_id=0, has_side_effects=True, vmem_limit_bytes=52 << 20

time: 55.7 us -> 53.4 us (0.959)
  Pallas kernels: 55 us -> 52.2 us
    pallas_call x1, Pallas kernels: 52.8 us -> 50 us  [per_device(): pl.pallas_call(kernel, name='diloco_step', out_shape=tuple((pltpu.VMEM(*o...]
where the time goes in v3:
time: 53.4 us; the launch traced here: 52.8 us
  Pallas kernels  52.2 us (98%)
  between operations  0.64 us (1%)
    pallas_call x1, Pallas kernels, per_device(): pl.pallas_call(kernel, name='diloco_step', out_shape=tuple((pltpu.VMEM(*o...  50 us
    pallas_call x1, Pallas kernels, per_device(): pl.pallas_call(write_out, name='write_out', out_shape=tuple((jax.ShapeDty...  2.15 us

profile of v3, /device:TPU:2, one launch (start us, length us, event | category | flops | bytes accessed | tf_op | source)
XLA Modules:
  0.0 52.8 jit_solution(4017648040855309488)
XLA Ops:
  0.6 50.0 %diloco_step.1 = (bf16[2,128,512]{2,1,0:T(8,128)(2,1)S(1)}, f32[4,8,32,512]{3,2,1,0:T(8,128)S(1)}, f32[4,8,32,512]{3,2,1,0:T(8,128)S(1)}, f32[16,512]{1,0:T(8,128)S(1)}, f32[16,512]{1,0:T(8,128)S(1)}) custom-call(bf16[256,4096]{1,0:T(8,128)(2,1)} %bitcast.9, f32[1,4096]{1,0:T(1,128)} %bitcast.17, bf16[4,8,32,512]{3,2,1,0:T(8,128)(2,1)} %bitcast.14, ...), custom_call_target="tpu_custom_call" | custom-call | flops 2147483648 | bytes 12582912 | tf_op jit(solution)/shard_map/diloco_step/pallas_call | solution.py:355
  50.7 2.1 %write_out.1 = (bf16[2,128,512]{2,1,0:T(8,128)(2,1)}, f32[4,8,32,512]{3,2,1,0:T(8,128)}, f32[4,8,32,512]{3,2,1,0:T(8,128)}, f32[16,512]{1,0:T(8,128)}, f32[16,512]{1,0:T(8,128)}) custom-call(bf16[2,128,512]{2,1,0:T(8,128)(2,1)S(1)} %get-tuple-element.15.refs_0_, f32[4,8,32,512]{3,2,1,0:T(8,128)S(1)} %get-tuple-element.16.refs_1_, ...), custom_call_target="tpu_custom_call" | custom-call | bytes 5242880 | tf_op jit(solution)/shard_map/write_out/pallas_call | solution.py:413

commit v4 on v3

--- a/solution.py
+++ b/solution.py
@@ -21,7 +21,7 @@
 AHEAD = 3
 LAG = 2
 KV = 512
-PIECES = 2
+PIECES = 1
 PK = KV // PIECES
 
 
@@ -283,8 +283,8 @@
     take_half(0)
     last_partial(0)
     sum_y(5)
+    to_partner(0)
     take_half(1)
-    to_partner(0)
     inner_step(7, last=True)
     last_partial(1)
     sum_y(6)

time: 53.4 us -> 53.1 us (level)
  no operation moved by 1% of the time
where the time goes in v4:
time: 53.1 us; the launch traced here: 52.7 us
  Pallas kernels  52.1 us (98%)
  between operations  0.64 us (1%)
    pallas_call x1, Pallas kernels, per_device(): pl.pallas_call(kernel, name='diloco_step', out_shape=tuple((pltpu.VMEM(*o...  49.9 us
    pallas_call x1, Pallas kernels, per_device(): pl.pallas_call(write_out, name='write_out', out_shape=tuple((jax.ShapeDty...  2.15 us

profile of v4, /device:TPU:2, one launch (start us, length us, event | category | flops | bytes accessed | tf_op | source)
XLA Modules:
  0.0 52.7 jit_solution(5307040561443501326)
XLA Ops:
  0.6 49.9 %diloco_step.1 = (bf16[2,128,512]{2,1,0:T(8,128)(2,1)S(1)}, f32[4,8,32,512]{3,2,1,0:T(8,128)S(1)}, f32[4,8,32,512]{3,2,1,0:T(8,128)S(1)}, f32[16,512]{1,0:T(8,128)S(1)}, f32[16,512]{1,0:T(8,128)S(1)}) custom-call(bf16[256,4096]{1,0:T(8,128)(2,1)} %bitcast.9, f32[1,4096]{1,0:T(1,128)} %bitcast.17, bf16[4,8,32,512]{3,2,1,0:T(8,128)(2,1)} %bitcast.14, ...), custom_call_target="tpu_custom_call" | custom-call | flops 2147483648 | bytes 12582912 | tf_op jit(solution)/shard_map/diloco_step/pallas_call | solution.py:355
  50.6 2.1 %write_out.1 = (bf16[2,128,512]{2,1,0:T(8,128)(2,1)}, f32[4,8,32,512]{3,2,1,0:T(8,128)}, f32[4,8,32,512]{3,2,1,0:T(8,128)}, f32[16,512]{1,0:T(8,128)}, f32[16,512]{1,0:T(8,128)}) custom-call(bf16[2,128,512]{2,1,0:T(8,128)(2,1)S(1)} %get-tuple-element.15.refs_0_, f32[4,8,32,512]{3,2,1,0:T(8,128)S(1)} %get-tuple-element.16.refs_1_, ...), custom_call_target="tpu_custom_call" | custom-call | bytes 5242880 | tf_op jit(solution)/shard_map/write_out/pallas_call | solution.py:413

commit v5 on v4

--- a/solution.py
+++ b/solution.py
@@ -293,9 +293,17 @@
     def add_z(k, total):
         return total + zrecv[k]
 
+    base = sum_weights(z)
+    for cp in [cot_p, cot_s, cot_f]:
+        cp.wait_send()
+    arrived(wv.at[0:3], w_ss)
+    arrived(nts, x_ss)
+    arrived(yrecv.at[:, 0:3], y_ss)
+    loads["anc"].wait()
+    loads["mom"].wait()
     arrived(zrecv, z_rs)
 
-    total = lax.fori_loop(0, 7, add_z, sum_weights(z))
+    total = lax.fori_loop(0, 7, add_z, base)
     xown[...] = total
     cp_xl = remote(xown.at[1 - xl], xrecv, xl_ss, xl_rs, at_xl)
     cp_xl.start()
@@ -313,8 +321,6 @@
 
     finish(0)
     cp_xl.wait_recv()
-    loads["anc"].wait()
-    loads["mom"].wait()
     steps = ysend[7, y, xl].astype(F32)
     arrived(ysend.at[0:7, 0, 0], yl_rs)
     for d, e in last_to:
@@ -325,11 +331,7 @@
     ancn[...] = ancv[...] - outer_rate * (nesterov_mu * new_momentum + mean_delta)
     finish(1)
 
-    for cp in [cot_p, cot_s, cot_f, cp_xl]:
-        cp.wait_send()
-    arrived(wv.at[0:3], w_ss)
-    arrived(nts, x_ss)
-    arrived(yrecv.at[:, 0:3], y_ss)
+    cp_xl.wait_send()
     arrived(ysend.at[0:7, 0, 0], yl_ss)
     arrived(zsend, z_ss)
     arrived(sib, sib_ss)

time: 53.1 us -> 53.1 us (level)
  no operation moved by 1% of the time
where the time goes in v5:
time: 53.1 us; the launch traced here: 52.7 us
  Pallas kernels  52.1 us (98%)
  between operations  0.64 us (1%)
    pallas_call x1, Pallas kernels, per_device(): pl.pallas_call(kernel, name='diloco_step', out_shape=tuple((pltpu.VMEM(*o...  49.9 us
    pallas_call x1, Pallas kernels, per_device(): pl.pallas_call(write_out, name='write_out', out_shape=tuple((jax.ShapeDty...  2.15 us

profile of v5, /device:TPU:2, one launch (start us, length us, event | category | flops | bytes accessed | tf_op | source)
XLA Modules:
  0.0 52.7 jit_solution(2460573584331148721)
XLA Ops:
  0.6 49.9 %diloco_step.1 = (bf16[2,128,512]{2,1,0:T(8,128)(2,1)S(1)}, f32[4,8,32,512]{3,2,1,0:T(8,128)S(1)}, f32[4,8,32,512]{3,2,1,0:T(8,128)S(1)}, f32[16,512]{1,0:T(8,128)S(1)}, f32[16,512]{1,0:T(8,128)S(1)}) custom-call(bf16[256,4096]{1,0:T(8,128)(2,1)} %bitcast.9, f32[1,4096]{1,0:T(1,128)} %bitcast.17, bf16[4,8,32,512]{3,2,1,0:T(8,128)(2,1)} %bitcast.14, ...), custom_call_target="tpu_custom_call" | custom-call | flops 2147483648 | bytes 12582912 | tf_op jit(solution)/shard_map/diloco_step/pallas_call | solution.py:357
  50.6 2.1 %write_out.1 = (bf16[2,128,512]{2,1,0:T(8,128)(2,1)}, f32[4,8,32,512]{3,2,1,0:T(8,128)}, f32[4,8,32,512]{3,2,1,0:T(8,128)}, f32[16,512]{1,0:T(8,128)}, f32[16,512]{1,0:T(8,128)}) custom-call(bf16[2,128,512]{2,1,0:T(8,128)(2,1)S(1)} %get-tuple-element.15.refs_0_, f32[4,8,32,512]{3,2,1,0:T(8,128)S(1)} %get-tuple-element.16.refs_1_, ...), custom_call_target="tpu_custom_call" | custom-call | bytes 5242880 | tf_op jit(solution)/shard_map/write_out/pallas_call | solution.py:415
